TPU v7x, 32 devices: a whole 2x2x4 slice. The times are simulated.
32 devices in a mesh: dom: 16 (over z, y, core), col: 2 (over x).
Axes of the slice: x: 2, y: 2, z: 4, core: 2. Of those that a mesh axis runs over, the one named last changes fastest.
Arguments:
- feats_t: bfloat16 [256, 32768], P('col', 'dom'), may hold values from -6 to 6
- weight: bfloat16 [256, 256], P('col'), may hold values from -0.375 to 0.375
- cotangent_t: bfloat16 [256, 32768], P('col', 'dom'), may hold values from -6 to 6
- tiles: bfloat16 [256, 8, 128, 128], P('dom'), may hold values from 0 to 0.1045825
- tile_cols: int32 [256, 8], P('dom'), may hold values from 0 to 79
- tile_count: int32 [256], P('dom'), may hold values from 5 to 8, as said below
- send_blocks: int32 [16, 8, 8], P('dom'), may hold values from 0 to 15, as said below
Outputs:
- output_t: bfloat16 [256, 32768], P('col', 'dom')
- grad_weight: float32 [256, 256], P('col')
- grad_feats_t: float32 [256, 32768], P('col', 'dom')
Inputs may be any that keep to these rules, and one draw needn't show every extreme that they name: Slots from tile_count onward are padding and are not part of the adjacency. `send_blocks`: within one partition and round the 8 listed blocks are different.
All inputs are finite; a program needn't handle non-finite values.
Results may differ from a plain program's by a relative error of at most 0.0056.
Values may be sent and summed in bfloat16 or wider, within the bound.
A program may use at most 64 MiB of HBM per device.

v0:
```python
import jax
import jax.numpy as jnp
from jax import lax
from jax.sharding import PartitionSpec as P


def shifted(block, axis, distance):
    devices = range(lax.axis_size(axis))
    route = [((i - distance) % len(devices), i) for i in devices]
    return lax.ppermute(block, axis, route)


def round_offset(round_index):
    step_size = round_index // 2 + 1
    return step_size if round_index % 2 == 0 else -step_size


def silu_slope(values):
    sigma = jax.nn.sigmoid(values)
    return sigma * (1.0 + values * (1.0 - sigma))


def aggregate(ext_rows, slot_cols, slot_mask, tiles):
    feature_count = ext_rows.shape[0]
    block_count, slot_total = slot_cols.shape
    block_size = ext_rows.shape[2]
    picked = jnp.take(ext_rows, slot_cols.reshape(-1), axis=1).reshape(
        feature_count, block_count, slot_total, block_size
    )
    picked = jnp.where(slot_mask[None, :, :, None], picked, jnp.zeros_like(picked))
    return jnp.einsum("fbtc,btrc->fbr", picked, tiles, preferred_element_type=jnp.float32)


def shards(feats_t, weight, cotangent_t, tiles, tile_cols, tile_count, send_blocks):
    feature_count, node_count = feats_t.shape
    block_size = tiles.shape[2]
    block_count = node_count // block_size
    slot_total = tiles.shape[1]
    round_total = send_blocks.shape[1]
    per_round = send_blocks.shape[2]
    ext_total = block_count + round_total * per_round
    own_blocks = feats_t.reshape(feature_count, block_count, block_size)
    slot_mask = jnp.arange(slot_total, dtype=jnp.int32)[None, :] < tile_count[:, None]
    send_lists = send_blocks[0]
    received = [own_blocks]
    for round_index in range(round_total):
        outgoing = jnp.take(own_blocks, send_lists[round_index], axis=1)
        received.append(shifted(outgoing, "dom", round_offset(round_index)))
    ext_rows = jnp.concatenate(received, axis=1)
    summed = aggregate(ext_rows, tile_cols, slot_mask, tiles)
    aggregated = summed.reshape(feature_count, node_count).astype(jnp.bfloat16)
    weight_cols = weight
    pre_act = lax.psum_scatter(
        jnp.einsum("io,in->on", weight_cols, aggregated, preferred_element_type=jnp.float32),
        "col",
        scatter_dimension=0,
        tiled=True,
    )
    output_t = jax.nn.silu(pre_act).astype(jnp.bfloat16)
    grad_pre = (cotangent_t.astype(jnp.float32) * silu_slope(pre_act)).astype(jnp.bfloat16)
    back_piece = lax.all_gather(grad_pre, "col", axis=0, tiled=True)
    weight_cols = weight
    block_grad = jnp.einsum("in,on->io", aggregated, back_piece, preferred_element_type=jnp.float32)
    weight_part = block_grad
    agg_part = jnp.einsum("io,on->in", weight_cols, back_piece, preferred_element_type=jnp.float32)
    weight_part, agg_part = (weight_part, agg_part)
    grad_weight = lax.psum(weight_part, "dom")
    grad_agg = agg_part.astype(jnp.bfloat16).reshape(feature_count, block_count, block_size)
    terms = jnp.einsum("fbr,btrc->fbtc", grad_agg, tiles, preferred_element_type=jnp.float32)
    terms = jnp.where(slot_mask[None, :, :, None], terms, 0.0)
    ext_grad = jnp.zeros((feature_count, ext_total, block_size), jnp.float32)
    ext_grad = ext_grad.at[:, tile_cols.reshape(-1)].add(
        terms.reshape(feature_count, block_count * slot_total, block_size)
    )
    grad_own = ext_grad[:, :block_count]
    for round_index in range(round_total):
        lower = block_count + round_index * per_round
        piece = ext_grad[:, lower : lower + per_round]
        back_rows = shifted(piece.astype(jnp.bfloat16), "dom", -round_offset(round_index)).astype(
            piece.dtype
        )
        grad_own = grad_own.at[:, send_lists[round_index]].add(back_rows)
    grad_feats_t = grad_own.reshape(feature_count, node_count)
    return (output_t, grad_weight, grad_feats_t)


def solution(mesh):
    placed = (
        P("col", "dom"),
        P("col", None),
        P("col", "dom"),
        P("dom", None, None, None),
        P("dom", None),
        P("dom"),
        P("dom", None, None),
    )
    return jax.shard_map(
        shards,
        mesh=mesh,
        in_specs=placed,
        out_specs=(P("col", "dom"), P("col", None), P("col", "dom")),
        check_vma=False,
    )
```

profile of v0, /device:TPU:0, one launch (start us, length us, event | category | flops | bytes accessed | tf_op | source)
XLA Modules:
  0.0 267.4 jit_solution(5198732622761795107)
XLA Ops:
  7.2 1.3 copy.24
  12.5 5.0 %collective-permute-start.1 = (bf16[128,8,128]{2,0,1:T(8,128)(2,1)}, bf16[128,8,128]{2,0,1:T(8,128)(2,1)}, u32[]{:S(2)}, u32[]{:S(2)}) collective-permute-start(bf16[128,8,128]{2,0,1:T(8,128)(2,1)} %select_bitcast_fusion.6), channel_id=1, source_target_pairs={{2,0},{4,2},{6,4},{8,6},{10,8},{12,10},{14,12},{16,14},{18,16},{20... | collective-permute-start | bytes 786440 | tf_op jit(solution)/shard_map/ppermute | solution.py:10
  20.3 4.7 %collective-permute-start.3 = (bf16[128,8,128]{2,0,1:T(8,128)(2,1)}, bf16[128,8,128]{2,0,1:T(8,128)(2,1)}, u32[]{:S(2)}, u32[]{:S(2)}) collective-permute-start(bf16[128,8,128]{2,0,1:T(8,128)(2,1)} %select_bitcast_fusion.4), channel_id=1, source_target_pairs={{4,0},{6,2},{8,4},{10,6},{12,8},{14,10},{16,12},{18,14},{20,16},{2... | collective-permute-start | bytes 786440 | tf_op jit(solution)/shard_map/ppermute | solution.py:10
  31.1 3.6 %collective-permute-start.5 = (bf16[128,8,128]{2,0,1:T(8,128)(2,1)}, bf16[128,8,128]{2,0,1:T(8,128)(2,1)S(1)}, u32[]{:S(2)}, u32[]{:S(2)}) collective-permute-start(bf16[128,8,128]{2,0,1:T(8,128)(2,1)} %select_bitcast_fusion.2), channel_id=1, source_target_pairs={{6,0},{8,2},{10,4},{12,6},{14,8},{16,10},{18,12},{20,14},{22,16},{... | collective-permute-start | bytes 786440 | tf_op jit(solution)/shard_map/ppermute | solution.py:10
  36.7 3.9 %collective-permute-start.7 = (bf16[128,8,128]{2,0,1:T(8,128)(2,1)}, bf16[128,8,128]{2,0,1:T(8,128)(2,1)S(1)}, u32[]{:S(2)}, u32[]{:S(2)}) collective-permute-start(bf16[128,8,128]{2,0,1:T(8,128)(2,1)} %select_bitcast_fusion), channel_id=1, source_target_pairs={{8,0},{10,2},{12,4},{14,6},{16,8},{18,10},{20,12},{22,14},{24,16},... | collective-permute-start | bytes 786440 | tf_op jit(solution)/shard_map/ppermute | solution.py:10
  43.6 3.7 %collective-permute-done.6 = bf16[128,8,128]{2,0,1:T(8,128)(2,1)S(1)} collective-permute-done((bf16[128,8,128]{2,0,1:T(8,128)(2,1)}, bf16[128,8,128]{2,0,1:T(8,128)(2,1)S(1)}, u32[]{:S(2)}, u32[]{:S(2)}) %collective-permute-start.6) | collective-permute-done | bytes 262176 | tf_op jit(solution)/shard_map/ppermute | solution.py:10
  47.4 3.7 %collective-permute-done.7 = bf16[128,8,128]{2,0,1:T(8,128)(2,1)S(1)} collective-permute-done((bf16[128,8,128]{2,0,1:T(8,128)(2,1)}, bf16[128,8,128]{2,0,1:T(8,128)(2,1)S(1)}, u32[]{:S(2)}, u32[]{:S(2)}) %collective-permute-start.7) | collective-permute-done | bytes 262176 | tf_op jit(solution)/shard_map/ppermute | solution.py:10
  51.1 3.0 %gather_fusion = bf16[128,128,128]{2,1,0:T(8,128)(2,1)} fusion(bf16[128,80,128]{2,0,1:T(8,128)(2,1)S(1)} %constant_dynamic-update-slice_fusion, s32[1024]{0:T(1024)S(1)} %pad_clamp_fusion), kind=kCustom, calls=%fused_computation.8 | custom fusion | bytes 8389120 | tf_op jit(solution)/shard_map/jit(_take)/gather | solution.py:27
  54.2 4.8 %fusion.10 = bf16[16,128,128]{1,2,0:T(8,128)(2,1)S(1)} fusion(bf16[16,8,128,128]{3,2,1,0:T(8,128)(2,1)} %param.12, bf16[128,16,8,128]{3,0,2,1:T(8,128)(2,1)} %bitcast.127, pred[16,8]{1,0:T(8,128)(4,1)S(1)} %copy.23, pred[16,8]{1,0:T(8,128)(4,1)S(1)} %iota_compare_fusion), kind=kOutput, calls=%fused_computation.29 | convolution fusion | flops 541327360 | bytes 8913152 | tf_op jit(solution)/shard_map/fbtc,btrc->fbr/dot_general | solution.py:31
  59.0 1.8 convolution_bitcast_fusion
  61.2 31.7 %reduce-scatter.2.cloned.1.call-done = f32[128,2048]{0,1:T(8,128)} async-done(((f32[256,2048]{0,1:T(8,128)}), f32[128,2048]{0,1:T(8,128)}) %reduce-scatter.2.cloned.1.call-update) | async-done | bytes 1048592 | tf_op jit(solution)/shard_map/reduce_scatter | solution.py:53
  92.8 2.5 multiply_convert_fusion
  96.5 20.4 %all-gather.2.cloned.1.call-done = bf16[256,2048]{0,1:T(8,128)(2,1)} async-done(((bf16[128,2048]{0,1:T(8,128)(2,1)}), bf16[256,2048]{0,1:T(8,128)(2,1)}) %all-gather.2.cloned.1.call-update) | async-done | bytes 1048592 | tf_op jit(solution)/shard_map/all_gather | solution.py:61
  116.8 1.7 convolution_convert_fusion
  118.5 6.8 %broadcast_select_fusion = f32[16,128,8,128]{3,1,2,0:T(8,128)} fusion(pred[16,8]{1,0:T(8,128)(4,1)S(1)} %iota_compare_fusion, bf16[128,16,128,1]{0,2,3,1:T(8,128)(2,1)S(1)} %bitcast.129, bf16[16,8,128,128]{3,2,1,0:T(8,128)(2,1)} %param.12), kind=kOutput, calls=%fused_computation.18 | convolution fusion | flops 538968064 | bytes 13107328 | tf_op jit(solution)/shard_map/fbr,btrc->fbtc/dot_general | solution.py:69
  125.3 3.0 %broadcast_in_dim.62 = f32[128,80,128]{2,0,1:T(8,128)} broadcast(f32[]{:T(128)} %constant.23.clone.1), dimensions={} | broadcast | bytes 5242884 | tf_op jit(solution)/shard_map/broadcast_in_dim | solution.py:71
  128.3 26.8 %scatter_fusion = f32[128,80,128]{2,0,1:T(8,128)} fusion(f32[128,80,128]{2,0,1:T(8,128)} %broadcast_in_dim.62, s32[128]{0:T(128)S(1)} %fusion.13, f32[128,128,128]{2,1,0:T(8,128)} %bitcast.126), kind=kCustom, calls=%fused_computation.9 | custom fusion | flops 2097152 | bytes 25166336 | tf_op jit(solution)/shard_map/scatter-add | solution.py:72
  155.1 3.0 %convert.10 = bf16[128,80,128]{2,0,1:T(8,128)(2,1)S(1)} convert(f32[128,80,128]{2,0,1:T(8,128)} %scatter_fusion) | non-fusion elementwise | flops 1310720 | bytes 7864320 | tf_op jit(solution)/shard_map/convert.7
  159.1 3.5 %collective-permute-start.8 = (bf16[128,8,128]{2,0,1:T(8,128)(2,1)S(1)}, bf16[128,8,128]{2,0,1:T(8,128)(2,1)S(1)}, u32[]{:S(2)}, u32[]{:S(2)}) collective-permute-start(bf16[128,8,128]{2,0,1:T(8,128)(2,1)S(1)} %get-tuple-element.36), channel_id=1, source_target_pairs={{2,0},{4,2},{6,4},{8,6},{10,8},{12,10},{14,12},{16,14},{18,16},{20... | collective-permute-start | bytes 786440 | tf_op jit(solution)/shard_map/ppermute | solution.py:10
  163.6 1.3 slice.110
  165.0 1.4 collective-permute-start.10
  167.0 2.8 %collective-permute-start.12 = (bf16[128,8,128]{2,0,1:T(8,128)(2,1)}, bf16[128,8,128]{2,0,1:T(8,128)(2,1)S(1)}, u32[]{:S(2)}, u32[]{:S(2)}) collective-permute-start(bf16[128,8,128]{2,0,1:T(8,128)(2,1)} %get-tuple-element.32), channel_id=1, source_target_pairs={{6,0},{8,2},{10,4},{12,6},{14,8},{16,10},{18,12},{20,14},{22,16},{... | collective-permute-start | bytes 786440 | tf_op jit(solution)/shard_map/ppermute | solution.py:10
  169.8 1.4 collective-permute-done.9
  171.3 3.0 %collective-permute-start.14 = (bf16[128,8,128]{2,0,1:T(8,128)(2,1)}, bf16[128,8,128]{2,0,1:T(8,128)(2,1)S(1)}, u32[]{:S(2)}, u32[]{:S(2)}) collective-permute-start(bf16[128,8,128]{2,0,1:T(8,128)(2,1)} %get-tuple-element.30), channel_id=1, source_target_pairs={{8,0},{10,2},{12,4},{14,6},{16,8},{18,10},{20,12},{22,14},{24,16},... | collective-permute-start | bytes 786440 | tf_op jit(solution)/shard_map/ppermute | solution.py:10
  174.3 9.1 %collective-permute-done.10 = bf16[128,8,128]{2,0,1:T(8,128)(2,1)S(1)} collective-permute-done((bf16[128,8,128]{2,0,1:T(8,128)(2,1)S(1)}, bf16[128,8,128]{2,0,1:T(8,128)(2,1)S(1)}, u32[]{:S(2)}, u32[]{:S(2)}) %collective-permute-start.10) | collective-permute-done | bytes 262176 | tf_op jit(solution)/shard_map/ppermute | solution.py:10
  183.6 1.4 collective-permute-done.12
  187.5 7.2 %collective-permute-done.15 = bf16[128,8,128]{2,0,1:T(8,128)(2,1)S(1)} collective-permute-done((bf16[128,8,128]{2,0,1:T(8,128)(2,1)S(1)}, bf16[128,8,128]{2,0,1:T(8,128)(2,1)S(1)}, u32[]{:S(2)}, u32[]{:S(2)}) %collective-permute-start.15) | collective-permute-done | bytes 262176 | tf_op jit(solution)/shard_map/ppermute | solution.py:10
  197.6 1.0 scatter_fusion.3
  198.7 1.0 scatter_fusion.4
  204.3 1.3 copy.39
  205.6 53.7 %all-reduce.2.cloned.1.call-done = f32[128,256]{1,0:T(8,128)} async-done(((f32[128,256]{1,0:T(8,128)}), f32[128,256]{1,0:T(8,128)}) %all-reduce.2.cloned.1.call-update) | async-done | bytes 131088 | tf_op jit(solution)/shard_map/psum | solution.py:67
  259.4 1.6 copy.62
  (106 shorter events, 32.0 us)
Async XLA Ops:
  7.2 51.9 %copy-start = (bf16[128,256]{1,0:T(8,128)(2,1)S(1)}, bf16[128,256]{1,0:T(8,128)(2,1)}, u32[]{:S(2)}) copy-start(bf16[128,256]{1,0:T(8,128)(2,1)} %param.10) | copy-start | bytes 196612
  7.2 85.6 %reduce-scatter.2.cloned.1.call-start = ((), (), s32[]{:S(2)}) async-start(), calls=%async_computation.1 | async-start | bytes 3145728 | tf_op jit(solution)/shard_map/reduce_scatter | solution.py:53
  9.8 16.6 %copy-start.7 = (s32[16,8]{0,1:T(8,128)S(1)}, s32[16,8]{0,1:T(8,128)}, u32[]{:S(2)}) copy-start(s32[16,8]{0,1:T(8,128)} %param.13) | copy-start | bytes 1540
  10.6 20.5 %collective-permute-start = (bf16[128,8,128]{2,0,1:T(8,128)(2,1)S(1)}, bf16[128,8,128]{2,0,1:T(8,128)(2,1)}, u32[]{:S(2)}, u32[]{:S(2)}) collective-permute-start(bf16[128,8,128]{2,0,1:T(8,128)(2,1)S(1)} %select_bitcast_fusion.7), channel_id=1, source_target_pairs={{30,0},{0,2},{2,4},{4,6},{6,8},{8,10},{10,12},{12,14},{14,16},{16,... | collective-permute-start | bytes 786440 | tf_op jit(solution)/shard_map/ppermute | solution.py:10
  11.7 16.8 %copy-start.9 = (s32[16]{0:T(128)S(1)}, s32[16]{0:T(128)}, u32[]{:S(2)}) copy-start(s32[16]{0:T(128)} %param.14) | copy-start | bytes 196
  12.5 23.2 %collective-permute-start.1 = (bf16[128,8,128]{2,0,1:T(8,128)(2,1)}, bf16[128,8,128]{2,0,1:T(8,128)(2,1)}, u32[]{:S(2)}, u32[]{:S(2)}) collective-permute-start(bf16[128,8,128]{2,0,1:T(8,128)(2,1)} %select_bitcast_fusion.6), channel_id=1, source_target_pairs={{2,0},{4,2},{6,4},{8,6},{10,8},{12,10},{14,12},{16,14},{18,16},{20... | collective-permute-start | bytes 786440 | tf_op jit(solution)/shard_map/ppermute | solution.py:10
  18.9 17.8 %collective-permute-start.2 = (bf16[128,8,128]{2,0,1:T(8,128)(2,1)}, bf16[128,8,128]{2,0,1:T(8,128)(2,1)}, u32[]{:S(2)}, u32[]{:S(2)}) collective-permute-start(bf16[128,8,128]{2,0,1:T(8,128)(2,1)} %select_bitcast_fusion.5), channel_id=1, source_target_pairs={{28,0},{30,2},{0,4},{2,6},{4,8},{6,10},{8,12},{10,14},{12,16},{14,... | collective-permute-start | bytes 786440 | tf_op jit(solution)/shard_map/ppermute | solution.py:10
  20.3 21.3 %collective-permute-start.3 = (bf16[128,8,128]{2,0,1:T(8,128)(2,1)}, bf16[128,8,128]{2,0,1:T(8,128)(2,1)}, u32[]{:S(2)}, u32[]{:S(2)}) collective-permute-start(bf16[128,8,128]{2,0,1:T(8,128)(2,1)} %select_bitcast_fusion.4), channel_id=1, source_target_pairs={{4,0},{6,2},{8,4},{10,6},{12,8},{14,10},{16,12},{18,14},{20,16},{2... | collective-permute-start | bytes 786440 | tf_op jit(solution)/shard_map/ppermute | solution.py:10
  26.4 16.1 %collective-permute-start.4 = (bf16[128,8,128]{2,0,1:T(8,128)(2,1)}, bf16[128,8,128]{2,0,1:T(8,128)(2,1)}, u32[]{:S(2)}, u32[]{:S(2)}) collective-permute-start(bf16[128,8,128]{2,0,1:T(8,128)(2,1)} %select_bitcast_fusion.3), channel_id=1, source_target_pairs={{26,0},{28,2},{30,4},{0,6},{2,8},{4,10},{6,12},{8,14},{10,16},{12,... | collective-permute-start | bytes 786440 | tf_op jit(solution)/shard_map/ppermute | solution.py:10
  31.1 12.5 %collective-permute-start.5 = (bf16[128,8,128]{2,0,1:T(8,128)(2,1)}, bf16[128,8,128]{2,0,1:T(8,128)(2,1)S(1)}, u32[]{:S(2)}, u32[]{:S(2)}) collective-permute-start(bf16[128,8,128]{2,0,1:T(8,128)(2,1)} %select_bitcast_fusion.2), channel_id=1, source_target_pairs={{6,0},{8,2},{10,4},{12,6},{14,8},{16,10},{18,12},{20,14},{22,16},{... | collective-permute-start | bytes 786440 | tf_op jit(solution)/shard_map/ppermute | solution.py:10
  35.7 11.7 %collective-permute-start.6 = (bf16[128,8,128]{2,0,1:T(8,128)(2,1)}, bf16[128,8,128]{2,0,1:T(8,128)(2,1)S(1)}, u32[]{:S(2)}, u32[]{:S(2)}) collective-permute-start(bf16[128,8,128]{2,0,1:T(8,128)(2,1)} %select_bitcast_fusion.1), channel_id=1, source_target_pairs={{24,0},{26,2},{28,4},{30,6},{0,8},{2,10},{4,12},{6,14},{8,16},{10,... | collective-permute-start | bytes 786440 | tf_op jit(solution)/shard_map/ppermute | solution.py:10
  36.7 14.4 %collective-permute-start.7 = (bf16[128,8,128]{2,0,1:T(8,128)(2,1)}, bf16[128,8,128]{2,0,1:T(8,128)(2,1)S(1)}, u32[]{:S(2)}, u32[]{:S(2)}) collective-permute-start(bf16[128,8,128]{2,0,1:T(8,128)(2,1)} %select_bitcast_fusion), channel_id=1, source_target_pairs={{8,0},{10,2},{12,4},{14,6},{16,8},{18,10},{20,12},{22,14},{24,16},... | collective-permute-start | bytes 786440 | tf_op jit(solution)/shard_map/ppermute | solution.py:10
  59.0 1.9 copy-start.6
  60.8 34.6 %copy-start.8 = (s32[1,8,8]{2,1,0:T(8,128)S(1)}, s32[1,8,8]{2,1,0:T(8,128)}, u32[]{:S(2)}) copy-start(s32[1,8,8]{2,1,0:T(8,128)} %param.15) | copy-start | bytes 772
  60.8 56.0 %all-gather.2.cloned.1.call-start = ((), (), s32[]{:S(2)}) async-start(), calls=%async_computation.2 | async-start | bytes 1572864 | tf_op jit(solution)/shard_map/all_gather | solution.py:61
  95.4 164.0 %all-reduce.2.cloned.1.call-start = ((), (), s32[]{:S(2)}) async-start(), calls=%async_computation.3 | async-start | bytes 262144 | tf_op jit(solution)/shard_map/psum | solution.py:67
  158.1 4.5 %copy-start.1 = (bf16[256,2048]{0,1:T(8,128)(2,1)S(1)}, bf16[256,2048]{0,1:T(8,128)(2,1)}, u32[]{:S(2)}) copy-start(bf16[256,2048]{0,1:T(8,128)(2,1)} %all-gather.2.cloned.1.call-done) | copy-start | bytes 3145732
  159.1 10.7 %collective-permute-start.8 = (bf16[128,8,128]{2,0,1:T(8,128)(2,1)S(1)}, bf16[128,8,128]{2,0,1:T(8,128)(2,1)S(1)}, u32[]{:S(2)}, u32[]{:S(2)}) collective-permute-start(bf16[128,8,128]{2,0,1:T(8,128)(2,1)S(1)} %get-tuple-element.36), channel_id=1, source_target_pairs={{2,0},{4,2},{6,4},{8,6},{10,8},{12,10},{14,12},{16,14},{18,16},{20... | collective-permute-start | bytes 786440 | tf_op jit(solution)/shard_map/ppermute | solution.py:10
  162.6 8.6 %collective-permute-start.9 = (bf16[128,8,128]{2,0,1:T(8,128)(2,1)S(1)}, bf16[128,8,128]{2,0,1:T(8,128)(2,1)S(1)}, u32[]{:S(2)}, u32[]{:S(2)}) collective-permute-start(bf16[128,8,128]{2,0,1:T(8,128)(2,1)S(1)} %get-tuple-element.35), channel_id=1, source_target_pairs={{30,0},{0,2},{2,4},{4,6},{6,8},{8,10},{10,12},{12,14},{14,16},{16,... | collective-permute-start | bytes 786440 | tf_op jit(solution)/shard_map/ppermute | solution.py:10
  165.0 18.5 %collective-permute-start.10 = (bf16[128,8,128]{2,0,1:T(8,128)(2,1)S(1)}, bf16[128,8,128]{2,0,1:T(8,128)(2,1)S(1)}, u32[]{:S(2)}, u32[]{:S(2)}) collective-permute-start(bf16[128,8,128]{2,0,1:T(8,128)(2,1)S(1)} %get-tuple-element.34), channel_id=1, source_target_pairs={{4,0},{6,2},{8,4},{10,6},{12,8},{14,10},{16,12},{18,14},{20,16},{2... | collective-permute-start | bytes 786440 | tf_op jit(solution)/shard_map/ppermute | solution.py:10
  166.4 17.1 %collective-permute-start.11 = (bf16[128,8,128]{2,0,1:T(8,128)(2,1)S(1)}, bf16[128,8,128]{2,0,1:T(8,128)(2,1)S(1)}, u32[]{:S(2)}, u32[]{:S(2)}) collective-permute-start(bf16[128,8,128]{2,0,1:T(8,128)(2,1)S(1)} %get-tuple-element.33), channel_id=1, source_target_pairs={{28,0},{30,2},{0,4},{2,6},{4,8},{6,10},{8,12},{10,14},{12,16},{14,... | collective-permute-start | bytes 786440 | tf_op jit(solution)/shard_map/ppermute | solution.py:10
  167.0 17.9 %collective-permute-start.12 = (bf16[128,8,128]{2,0,1:T(8,128)(2,1)}, bf16[128,8,128]{2,0,1:T(8,128)(2,1)S(1)}, u32[]{:S(2)}, u32[]{:S(2)}) collective-permute-start(bf16[128,8,128]{2,0,1:T(8,128)(2,1)} %get-tuple-element.32), channel_id=1, source_target_pairs={{6,0},{8,2},{10,4},{12,6},{14,8},{16,10},{18,12},{20,14},{22,16},{... | collective-permute-start | bytes 786440 | tf_op jit(solution)/shard_map/ppermute | solution.py:10
  169.8 16.1 %collective-permute-start.13 = (bf16[128,8,128]{2,0,1:T(8,128)(2,1)}, bf16[128,8,128]{2,0,1:T(8,128)(2,1)S(1)}, u32[]{:S(2)}, u32[]{:S(2)}) collective-permute-start(bf16[128,8,128]{2,0,1:T(8,128)(2,1)} %get-tuple-element.31), channel_id=1, source_target_pairs={{26,0},{28,2},{30,4},{0,6},{2,8},{4,10},{6,12},{8,14},{10,16},{12,... | collective-permute-start | bytes 786440 | tf_op jit(solution)/shard_map/ppermute | solution.py:10
  171.3 15.4 %collective-permute-start.14 = (bf16[128,8,128]{2,0,1:T(8,128)(2,1)}, bf16[128,8,128]{2,0,1:T(8,128)(2,1)S(1)}, u32[]{:S(2)}, u32[]{:S(2)}) collective-permute-start(bf16[128,8,128]{2,0,1:T(8,128)(2,1)} %get-tuple-element.30), channel_id=1, source_target_pairs={{8,0},{10,2},{12,4},{14,6},{16,8},{18,10},{20,12},{22,14},{24,16},... | collective-permute-start | bytes 786440 | tf_op jit(solution)/shard_map/ppermute | solution.py:10
  183.5 11.2 %collective-permute-start.15 = (bf16[128,8,128]{2,0,1:T(8,128)(2,1)S(1)}, bf16[128,8,128]{2,0,1:T(8,128)(2,1)S(1)}, u32[]{:S(2)}, u32[]{:S(2)}) collective-permute-start(bf16[128,8,128]{2,0,1:T(8,128)(2,1)S(1)} %get-tuple-element.29), channel_id=1, source_target_pairs={{24,0},{26,2},{28,4},{30,6},{0,8},{2,10},{4,12},{6,14},{8,16},{10,... | collective-permute-start | bytes 786440 | tf_op jit(solution)/shard_map/ppermute | solution.py:10
  196.6 3.2 %copy-start.2 = (f32[8,128,128]{2,1,0:T(8,128)S(1)}, f32[8,128,128]{2,1,0:T(8,128)}, u32[]{:S(2)}) copy-start(f32[8,128,128]{2,1,0:T(8,128)} %convert_bitcast_fusion.3) | copy-start | bytes 1572868
  197.6 3.2 %copy-start.3 = (f32[8,128,128]{2,1,0:T(8,128)S(1)}, f32[8,128,128]{2,1,0:T(8,128)}, u32[]{:S(2)}) copy-start(f32[8,128,128]{2,1,0:T(8,128)} %convert_bitcast_fusion.2) | copy-start | bytes 1572868
  198.7 3.2 %copy-start.4 = (f32[8,128,128]{2,1,0:T(8,128)S(1)}, f32[8,128,128]{2,1,0:T(8,128)}, u32[]{:S(2)}) copy-start(f32[8,128,128]{2,1,0:T(8,128)} %convert_bitcast_fusion.1) | copy-start | bytes 1572868
  199.7 3.2 %copy-start.5 = (f32[8,128,128]{2,1,0:T(8,128)S(1)}, f32[8,128,128]{2,1,0:T(8,128)}, u32[]{:S(2)}) copy-start(f32[8,128,128]{2,1,0:T(8,128)} %convert_bitcast_fusion) | copy-start | bytes 1572868
Sparse Core Ops, SparseCore 0:
  60.9 31.8 reduce-scatter.1
  95.5 21.2 all-gather.1
  165.1 94.2 all-reduce.1
where the time goes:
time: 269 us; the launch traced here: 267 us
  waiting for transfers between devices  132 us (49%)
  other arithmetic  50.9 us (19%)
  starting transfers between devices  29.2 us (11%)
  local copies, waits for them, and re-layouts  24.5 us (9%)
  matrix products  16 us (6%)
  between operations  14.3 us (5%)
    psum x1, waiting for transfers between devices, shards(): grad_weight = lax.psum(weight_part, 'dom')  53.7 us
    reduce_scatter x1, waiting for transfers between devices, shards(): lax.psum_scatter(jnp.einsum('io,in->on', weight_cols, aggregated, preferr...  31.7 us
    ppermute x16, starting transfers between devices, shifted(): return lax.ppermute(block, axis, route)  29.1 us
    scatter-add x1, other arithmetic, shards(): ext_grad.at[:, tile_cols.reshape(-1)]  26.8 us
    ppermute x16, waiting for transfers between devices, shifted(): return lax.ppermute(block, axis, route)  26.6 us
    all_gather x1, waiting for transfers between devices, shards(): back_piece = lax.all_gather(grad_pre, 'col', axis=0, tiled=True)  20.4 us
    unnamed x34, local copies, waits for them, and re-layouts  10.6 us
    scatter-add x8, other arithmetic, shards(): grad_own = grad_own.at[:, send_lists[round_index]].add(back_rows)  8.28 us
  transfers between devices with their start and end apart: 19, of which 10 were waited for; matrix products, arithmetic and copies ran while one was open for 12% of the time, Pallas kernels for 0%

commit v1 on v0

v1 whole, which is shorter than its diff:
```python
import functools

import jax
import jax.numpy as jnp
from jax import lax
from jax.experimental import pallas as pl
from jax.experimental.pallas import tpu as pltpu
from jax.sharding import PartitionSpec as P

MESH = pl.DeviceIdType.MESH
CHUNKS = 4
BF = jnp.bfloat16
F32 = jnp.float32


def round_offset(round_index):
    step_size = round_index // 2 + 1
    return step_size if round_index % 2 == 0 else -step_size


def nt_dot(a, b):
    return lax.dot_general(a, b, (((1,), (1,)), ((), ())), preferred_element_type=F32)


def nn_dot(a, b):
    return lax.dot_general(a, b, (((1,), (0,)), ((), ())), preferred_element_type=F32)


def forward_kernel(
    cols, counts, lists, feats, cot_hbm, w_hbm, tiles_hbm,
    out_ref, gagg_ref, gw_ref,
    own, stage, ext, tiles, cot, w, wt, agg,
    z_send, z_recv, c_send, c_recv, w_send, w_recv, a_send, a_recv, local_sem,
):
    n_dom = lax.axis_size("dom")
    n_col = lax.axis_size("col")
    me = lax.axis_index("dom")
    c = lax.axis_index("col")
    rounds, per = lists.shape
    blocks, size = own.shape[0], own.shape[2]
    slots = tiles.shape[1]
    feat = own.shape[1]
    width = w.shape[0] * feat
    ext_total = blocks + rounds * per

    barrier = pltpu.get_barrier_semaphore()
    for r in range(rounds):
        target = lax.rem(me + round_offset(r) + n_dom, n_dom)
        pl.semaphore_signal(barrier, inc=1, device_id={"dom": target}, device_id_type=MESH)
    for d in range(1, n_col):
        target = lax.rem(c + d, n_col)
        pl.semaphore_signal(barrier, inc=1, device_id={"col": target}, device_id_type=MESH)

    load_tiles = pltpu.make_async_copy(tiles_hbm, tiles, local_sem.at[0])
    load_cot = pltpu.make_async_copy(cot_hbm, cot.at[c], local_sem.at[1])
    load_w = pltpu.make_async_copy(w_hbm, w.at[c], local_sem.at[2])
    load_w.start()
    load_cot.start()
    load_tiles.start()

    def split(b, carry):
        block = feats[:, pl.ds(pl.multiple_of(b * size, size), size)]
        own[b] = block
        ext[b] = block
        return carry

    lax.fori_loop(0, blocks, split, 0)
    ext[ext_total] = jnp.zeros((feat, size), BF)

    z_copies = []
    for r in range(rounds):
        target = lax.rem(me + round_offset(r) + n_dom, n_dom)
        for j in range(per):
            stage[r * per + j] = own[lists[r, j]]
        if r == 0:
            pl.semaphore_wait(barrier, rounds + n_col - 1)
        copy = pltpu.make_async_remote_copy(
            src_ref=stage.at[pl.ds(r * per, per)],
            dst_ref=ext.at[pl.ds(blocks + r * per, per)],
            send_sem=z_send.at[r], recv_sem=z_recv.at[r],
            device_id={"dom": target}, device_id_type=MESH,
        )
        copy.start()
        z_copies.append(copy)

    def col_copy(at, d, here, send_sem, recv_sem):
        return pltpu.make_async_remote_copy(
            src_ref=at(here), dst_ref=at(here), send_sem=send_sem, recv_sem=recv_sem,
            device_id={"col": lax.rem(c + d, n_col)}, device_id_type=MESH,
        )

    load_w.wait()
    for d in range(1, n_col):
        col_copy(lambda i: w.at[i], d, c, w_send.at[d - 1], w_recv.at[d - 1]).start()
    load_cot.wait()
    for d in range(1, n_col):
        col_copy(lambda i: cot.at[i], d, c, c_send.at[d - 1], c_recv.at[d - 1]).start()

    def col_wait(at, d, send_sem, recv_sem):
        there = lax.rem(c - d + n_col, n_col)
        col_copy(at, d, c, send_sem, recv_sem).wait_send()
        col_copy(at, d, there, send_sem, recv_sem).wait_recv()

    for d in range(1, n_col):
        col_wait(lambda i: w.at[i], d, w_send.at[d - 1], w_recv.at[d - 1])
    turned = w[...].reshape(width, -1).astype(F32).T.astype(BF)
    wt[...] = turned.reshape(wt.shape)

    load_tiles.wait()
    for copy in z_copies:
        copy.wait()

    step = blocks // CHUNKS
    span = step * size
    for i in range(CHUNKS):
        def one(k, carry):
            b = i * step + k
            count = counts[b]
            picked = jnp.concatenate(
                [ext[jnp.where(t < count, cols[b, t], ext_total)] for t in range(slots)], axis=1
            )
            rows = jnp.concatenate([tiles[b, t] for t in range(slots)], axis=1)
            total = nt_dot(picked, rows).astype(BF)
            agg[i, c, :, pl.ds(pl.multiple_of(k * size, size), size)] = total
            return carry

        lax.fori_loop(0, step, one, 0)
        for d in range(1, n_col):
            col_copy(lambda q: agg.at[i, q], d, c, a_send.at[i, d - 1], a_recv.at[i, d - 1]).start()

    for d in range(1, n_col):
        col_wait(lambda q: cot.at[q], d, c_send.at[d - 1], c_recv.at[d - 1])

    gw = jnp.zeros((feat, width), F32)
    for i in range(CHUNKS):
        for d in range(1, n_col):
            col_wait(lambda q: agg.at[i, q], d, a_send.at[i, d - 1], a_recv.at[i, d - 1])
        whole = agg[i].reshape(width, span)
        pre = nn_dot(wt[...].reshape(width, width), whole)
        sigma = jax.nn.sigmoid(pre)
        slope = sigma * (1.0 + pre * (1.0 - sigma))
        held = cot[:, :, i * span : (i + 1) * span].reshape(width, span).astype(F32)
        grad = (held * slope).astype(BF)
        mine = nn_dot(wt[c], whole)
        out_ref[:, i * span : (i + 1) * span] = (mine * jax.nn.sigmoid(mine)).astype(BF)
        back = nn_dot(w[c], grad).astype(BF)
        for k in range(step):
            gagg_ref[i * step + k] = back[:, k * size : (k + 1) * size]
        gw = gw + nt_dot(agg[i, c], grad)
    half = gw_ref.shape[1]
    for h in range(width // half):
        gw_ref[h * feat : (h + 1) * feat] = gw[:, h * half : (h + 1) * half]


def scatter_kernel(cols, counts, gagg, tiles, own_ref, ext_ref, acc):
    step = pl.program_id(0)
    per_step, slots = tiles.shape[0], tiles.shape[1]
    blocks = own_ref.shape[0]
    total = acc.shape[0] - 1

    @pl.when(step == 0)
    def _():
        acc[...] = jnp.zeros_like(acc)

    for k in range(per_step):
        b = step * per_step + k
        count = counts[b]
        grad = gagg[k]
        for t in range(slots):
            at = jnp.where(t < count, cols[b, t], total)
            acc[at] += nn_dot(grad, tiles[k, t])

    @pl.when(step == pl.num_programs(0) - 1)
    def _():
        own_ref[...] = acc[:blocks]
        ext_ref[...] = acc[blocks:total].astype(BF)


def return_kernel(
    reduce_here, lists, ext_hbm, own, gw,
    out_ref, gw_out,
    got0, got1, got2, got3, got4, got5, got6, got7, parts, sums,
    z_send, z_recv, p_send, p_recv, s_send, s_recv, local_sem,
):
    got = [got0, got1, got2, got3, got4, got5, got6, got7]
    n_dom = lax.axis_size("dom")
    me = lax.axis_index("dom")
    rounds, per = lists.shape
    blocks, feat, size = own.shape

    def peer(distance):
        return lax.rem(me + distance + n_dom, n_dom)

    barrier = pltpu.get_barrier_semaphore()
    if reduce_here:
        def greet(d, carry):
            pl.semaphore_signal(barrier, inc=1, device_id={"dom": peer(d)}, device_id_type=MESH)
            return carry

        lax.fori_loop(1, n_dom, greet, 0)
    else:
        for r in range(rounds):
            pl.semaphore_signal(
                barrier, inc=1, device_id={"dom": peer(round_offset(r))}, device_id_type=MESH
            )
    for r in range(rounds):
        got[r][per] = jnp.zeros((feat, size), BF)
    pl.semaphore_wait(barrier, n_dom - 1 if reduce_here else rounds)

    def part_copy(d, target_slot, source_slot):
        return pltpu.make_async_remote_copy(
            src_ref=gw.at[source_slot], dst_ref=parts.at[target_slot],
            send_sem=p_send.at[d], recv_sem=p_recv.at[d],
            device_id={"dom": peer(d)}, device_id_type=MESH,
        )

    def sum_copy(d, slot):
        return pltpu.make_async_remote_copy(
            src_ref=sums.at[slot], dst_ref=sums.at[slot],
            send_sem=s_send.at[d], recv_sem=s_recv.at[d],
            device_id={"dom": peer(d)}, device_id_type=MESH,
        )

    if reduce_here:
        def send_part(d, carry):
            part_copy(d, d, peer(d)).start()
            return carry

        lax.fori_loop(1, n_dom, send_part, 0)

    copies = []
    for r in range(rounds):
        copy = pltpu.make_async_remote_copy(
            src_ref=ext_hbm.at[pl.ds(r * per, per)],
            dst_ref=got[r].at[pl.ds(0, per)],
            send_sem=z_send.at[r], recv_sem=z_recv.at[r],
            device_id={"dom": peer(-round_offset(r))}, device_id_type=MESH,
        )
        copy.start()
        copies.append(copy)

    if reduce_here:
        def wait_part(d, total):
            part_copy(d, d, peer(d)).wait()
            return total + parts[d]

        sums[me] = lax.fori_loop(1, n_dom, wait_part, gw[me])

        def send_sum(d, carry):
            sum_copy(d, me).start()
            return carry

        lax.fori_loop(1, n_dom, send_sum, 0)

    for r in range(rounds):
        copies[r].wait()

        def add(b, carry):
            at = per
            for j in range(per):
                at = jnp.where(lists[r, j] == b, j, at)
            columns = pl.ds(pl.multiple_of(b * size, size), size)
            base = own[b] if r == 0 else out_ref[:, columns]
            out_ref[:, columns] = base + got[r][at].astype(F32)
            return carry

        lax.fori_loop(0, blocks, add, 0)

    if reduce_here:
        def wait_sum(d, carry):
            sum_copy(d, me).wait_send()
            sum_copy(d, peer(-d)).wait_recv()
            return carry

        lax.fori_loop(1, n_dom, wait_sum, 0)
        flat = sums[...].reshape(-1, sums.shape[2])
        feat_rows = gw_out.shape[0]
        half = sums.shape[2]
        for h in range(gw_out.shape[1] // half):
            gw_out[:, h * half : (h + 1) * half] = flat[h * feat_rows : (h + 1) * feat_rows]
    else:
        gw_out[...] = jnp.zeros_like(gw_out)


def shards(n_dom, n_col, feats_t, weight, cotangent_t, tiles, tile_cols, tile_count, send_blocks):
    feat, nodes = feats_t.shape
    width = feat * n_col
    blocks, slots, size, _ = tiles.shape
    rounds, per = send_blocks.shape[1:]
    extra = rounds * per
    lists = send_blocks[0]
    step = blocks // CHUNKS
    span = step * size
    vmem = pl.BlockSpec(memory_space=pltpu.VMEM)
    smem = pl.BlockSpec(memory_space=pltpu.SMEM)
    anywhere = pl.BlockSpec(memory_space=pl.ANY)
    dma = pltpu.SemaphoreType.DMA
    half = 128

    output_t, gagg, gw = pl.pallas_call(
        forward_kernel,
        out_shape=(
            jax.ShapeDtypeStruct((feat, nodes), BF),
            jax.ShapeDtypeStruct((blocks, feat, size), BF),
            jax.ShapeDtypeStruct((feat * (width // half), half), F32),
        ),
        in_specs=[smem, smem, smem, vmem, anywhere, anywhere, anywhere],
        out_specs=(vmem, vmem, vmem),
        scratch_shapes=[
            pltpu.VMEM((blocks, feat, size), BF),
            pltpu.VMEM((extra, feat, size), BF),
            pltpu.VMEM((blocks + extra + 1, feat, size), BF),
            pltpu.VMEM(tiles.shape, BF),
            pltpu.VMEM((n_col, feat, nodes), BF),
            pltpu.VMEM((n_col, feat, width), BF),
            pltpu.VMEM((n_col, feat, width), BF),
            pltpu.VMEM((CHUNKS, n_col, feat, span), BF),
            dma((rounds,)), dma((rounds,)),
            dma((n_col - 1,)), dma((n_col - 1,)),
            dma((n_col - 1,)), dma((n_col - 1,)),
            dma((CHUNKS, n_col - 1)), dma((CHUNKS, n_col - 1)),
            dma((3,)),
        ],
        compiler_params=pltpu.CompilerParams(
            collective_id=0, has_side_effects=True, vmem_limit_bytes=40 * 2**20
        ),
        name="forward",
    )(tile_cols, tile_count, lists, feats_t, cotangent_t, weight, tiles)

    per_step = blocks // CHUNKS
    own, ext = pl.pallas_call(
        scatter_kernel,
        grid=(CHUNKS,),
        out_shape=(
            jax.ShapeDtypeStruct((blocks, feat, size), F32),
            jax.ShapeDtypeStruct((extra, feat, size), BF),
        ),
        in_specs=[
            smem, smem,
            pl.BlockSpec((per_step, feat, size), lambda i: (i, 0, 0)),
            pl.BlockSpec((per_step, slots, size, size), lambda i: (i, 0, 0, 0)),
        ],
        out_specs=(
            pl.BlockSpec((blocks, feat, size), lambda i: (0, 0, 0)),
            pl.BlockSpec((extra, feat, size), lambda i: (0, 0, 0)),
        ),
        scratch_shapes=[pltpu.VMEM((blocks + extra + 1, feat, size), F32)],
        compiler_params=pltpu.CompilerParams(vmem_limit_bytes=32 * 2**20),
        name="scatter",
    )(tile_cols, tile_count, gagg, tiles)

    total_rows = feat * (width // half)
    reduce_here = total_rows % n_dom == 0 and (total_rows // n_dom) % 8 == 0
    rows = total_rows // n_dom if reduce_here else 8
    parts_n = n_dom if reduce_here else 1
    gw_in = gw.reshape(n_dom, rows, half) if reduce_here else jnp.zeros((1, 8, half), F32)
    grad_feats_t, grad_weight = pl.pallas_call(
        functools.partial(return_kernel, reduce_here),
        out_shape=(
            jax.ShapeDtypeStruct((feat, nodes), F32),
            jax.ShapeDtypeStruct((feat, width), F32),
        ),
        in_specs=[smem, anywhere, vmem, vmem],
        out_specs=(vmem, vmem),
        scratch_shapes=[pltpu.VMEM((per + 1, feat, size), BF)] * rounds
        + [
            pltpu.VMEM((parts_n, rows, half), F32),
            pltpu.VMEM((parts_n, rows, half), F32),
            dma((rounds,)), dma((rounds,)),
            dma((n_dom,)), dma((n_dom,)),
            dma((n_dom,)), dma((n_dom,)),
            dma((1,)),
        ],
        compiler_params=pltpu.CompilerParams(
            collective_id=1, has_side_effects=True, vmem_limit_bytes=24 * 2**20
        ),
        name="give_back",
    )(lists, ext, own, gw_in)
    if not reduce_here:
        summed = lax.psum(gw, "dom").reshape(width // half, feat, half)
        grad_weight = summed.transpose(1, 0, 2).reshape(feat, width)
    return (output_t, grad_weight, grad_feats_t)


def solution(mesh):
    placed = (
        P("col", "dom"),
        P("col", None),
        P("col", "dom"),
        P("dom", None, None, None),
        P("dom", None),
        P("dom"),
        P("dom", None, None),
    )
    return jax.shard_map(
        functools.partial(shards, mesh.shape["dom"], mesh.shape["col"]),
        mesh=mesh,
        in_specs=placed,
        out_specs=(P("col", "dom"), P("col", None), P("col", "dom")),
        check_vma=False,
    )
```

time: 269 us -> 106 us (0.39)
  waiting for transfers between devices: 132 us -> 0 us
  Pallas kernels: 0 us -> 95.1 us
  other arithmetic: 50.9 us -> 0 us
  starting transfers between devices: 29.2 us -> 0 us
  matrix products: 16 us -> 0 us
  local copies, waits for them, and re-layouts: 24.5 us -> 9.63 us
  between operations: 14.3 us -> 0.66 us
    pallas_call x0 -> x3, Pallas kernels: none -> 95.1 us  [the longest x1 50.7 us: shards(): pl.pallas_call(forward_kernel, out_shape=(jax.ShapeDtypeStruct((feat, nod...]
    psum x1 -> x0, waiting for transfers between devices: 53.7 us -> none  [shards(): grad_weight = lax.psum(weight_part, 'dom')]
    scatter-add x9 -> x0, other arithmetic: 35.1 us -> none  [the longest x1 26.8 us: shards(): ext_grad.at[:, tile_cols.reshape(-1)]]
    reduce_scatter x1 -> x0, waiting for transfers between devices: 31.7 us -> none  [shards(): lax.psum_scatter(jnp.einsum('io,in->on', weight_cols, aggregated, preferr...]
    ppermute x16 -> x0, starting transfers between devices: 29.1 us -> none  [shifted(): return lax.ppermute(block, axis, route)]
    ppermute x16 -> x0, waiting for transfers between devices: 26.6 us -> none  [shifted(): return lax.ppermute(block, axis, route)]
    all_gather x1 -> x0, waiting for transfers between devices: 20.4 us -> none  [shards(): back_piece = lax.all_gather(grad_pre, 'col', axis=0, tiled=True)]
    dot_general x5 -> x0, matrix products: 16 us -> none  [the longest x1 6.77 us: shards(): jnp.einsum('fbr,btrc->fbtc', grad_agg, tiles, preferred_element_type=jnp....]
  transfers between devices with their start and end apart: 19 -> 0, of which waited for: 10 -> 0; matrix products, arithmetic and copies ran while one was open for 12% -> 0% of each run, Pallas kernels for 0% -> 0%
where the time goes in v1:
time: 106 us; the launch traced here: 105 us
  Pallas kernels  95.1 us (90%)
  local copies, waits for them, and re-layouts  9.63 us (9%)
    pallas_call x1, Pallas kernels, shards(): pl.pallas_call(forward_kernel, out_shape=(jax.ShapeDtypeStruct((feat, nod...  50.7 us
    pallas_call x1, Pallas kernels, shards(): pl.pallas_call(functools.partial(return_kernel, reduce_here), out_shape=(...  41.3 us
    unnamed x16, local copies, waits for them, and re-layouts  9.63 us
    pallas_call x1, Pallas kernels, shards(): pl.pallas_call(scatter_kernel, grid=(CHUNKS,), out_shape=(jax.ShapeDtypeS...  3.15 us

profile of v1, /device:TPU:0, one launch (start us, length us, event | category | flops | bytes accessed | tf_op | source)
XLA Modules:
  0.0 105.4 jit_solution(13565756571277293447)
XLA Ops:
  0.6 0.8 copy.10.cols
  1.4 0.0 copy-start
  1.4 2.2 %copy-done = bf16[16,8,128,128]{3,2,1,0:T(8,128)(2,1)S(1)} copy-done((bf16[16,8,128,128]{3,2,1,0:T(8,128)(2,1)S(1)}, bf16[16,8,128,128]{3,2,1,0:T(8,128)(2,1)}, u32[]{:S(2)}) %copy-start) | copy-done | bytes 4194328
  3.6 0.0 copy-start.1
  3.6 1.0 copy-done.1
  4.6 0.0 copy-start.2
  4.6 1.0 copy-done.2
  5.7 0.0 copy-start.3
  5.7 0.8 copy-done.3
  6.5 0.0 copy-start.4
  6.5 0.7 copy-done.4
  7.2 0.0 copy-start.5
  7.2 0.7 copy-done.5
  7.8 50.7 %forward.1 = (bf16[128,2048]{1,0:T(8,128)(2,1)S(1)}, bf16[16,128,128]{2,1,0:T(8,128)(2,1)S(1)}, f32[256,128]{1,0:T(8,128)S(1)}) custom-call(s32[16,8]{1,0:T(8,128)S(1)} %copy.10.cols, s32[16]{0:T(128)S(1)} %copy-done.5, s32[8,8]{1,0:T(8,128)S(1)} %bitcast.3, bf16[128,2048]{1,0:T(8,128)(2,1)S(1)} %copy-done.1, bf16[128,2048]{1,0:T(8,128)(2,1)S(1)} %copy-done.2, ...), custom_call_target="tpu_custom_call" | custom-call | tf_op jit(solution)/shard_map/forward/pallas_call | solution.py:300
  58.5 3.2 %scatter.1 = (f32[16,128,128]{2,1,0:T(8,128)S(1)}, bf16[64,128,128]{2,1,0:T(8,128)(2,1)S(1)}) custom-call(s32[16,8]{1,0:T(8,128)S(1)} %copy.10.cols, s32[16]{0:T(128)S(1)} %copy-done.5, bf16[16,128,128]{2,1,0:T(8,128)(2,1)S(1)} %get-tuple-element.11.gagg, bf16[16,8,128,128]{3,2,1,0:T(8,128)(2,1)S(1)} %copy-done), custom_call_target="tpu_custom_call" | custom-call | tf_op jit(solution)/shard_map/scatter/pallas_call | solution.py:331
  61.7 41.3 %give_back.1 = (f32[128,2048]{1,0:T(8,128)S(1)}, f32[128,256]{1,0:T(8,128)S(1)}) custom-call(s32[8,8]{1,0:T(8,128)S(1)} %bitcast.4, bf16[64,128,128]{2,1,0:T(8,128)(2,1)S(1)} %get-tuple-element.12.ext_hbm, f32[16,128,128]{2,1,0:T(8,128)S(1)} %get-tuple-element.13.own, f32[16,16,128]{2,1,0:T(8,128)S(1)} %bitcast.2), custom_call_target="tpu_custom_call" | custom-call | tf_op jit(solution)/shard_map/give_back/pallas_call | solution.py:357
  102.9 0.8 copy.15
  103.7 0.7 copy.16
  104.4 1.0 copy.17
Async XLA Ops:
  1.4 2.2 %copy-start = (bf16[16,8,128,128]{3,2,1,0:T(8,128)(2,1)S(1)}, bf16[16,8,128,128]{3,2,1,0:T(8,128)(2,1)}, u32[]{:S(2)}) copy-start(bf16[16,8,128,128]{3,2,1,0:T(8,128)(2,1)} %tiles.1) | copy-start | bytes 12582916
  3.6 1.0 copy-start.1
  4.6 1.0 copy-start.2
  5.7 0.8 copy-start.3
  6.5 0.7 copy-start.4
  7.2 0.7 copy-start.5

commit v2 on v1

--- a/solution.py
+++ b/solution.py
@@ -9,6 +9,7 @@
 
 MESH = pl.DeviceIdType.MESH
 CHUNKS = 4
+LANES = 4
 BF = jnp.bfloat16
 F32 = jnp.float32
 
@@ -29,7 +30,7 @@
 def forward_kernel(
     cols, counts, lists, feats, cot_hbm, w_hbm, tiles_hbm,
     out_ref, gagg_ref, gw_ref,
-    own, stage, ext, tiles, cot, w, wt, agg,
+    own, stage, ext0, ext1, tiles, cot, w, wt, agg,
     z_send, z_recv, c_send, c_recv, w_send, w_recv, a_send, a_recv, local_sem,
 ):
     n_dom = lax.axis_size("dom")
@@ -42,6 +43,8 @@
     feat = own.shape[1]
     width = w.shape[0] * feat
     ext_total = blocks + rounds * per
+    part = feat // 2
+    exts = [ext0, ext1]
 
     barrier = pltpu.get_barrier_semaphore()
     for r in range(rounds):
@@ -61,27 +64,32 @@
     def split(b, carry):
         block = feats[:, pl.ds(pl.multiple_of(b * size, size), size)]
         own[b] = block
-        ext[b] = block
+        ext0[b] = block[:part]
+        ext1[b] = block[part:]
         return carry
 
     lax.fori_loop(0, blocks, split, 0)
-    ext[ext_total] = jnp.zeros((feat, size), BF)
-
-    z_copies = []
-    for r in range(rounds):
+    ext0[ext_total] = jnp.zeros((part, size), BF)
+    ext1[ext_total] = jnp.zeros((part, size), BF)
+
+    def z_copy(h, r):
         target = lax.rem(me + round_offset(r) + n_dom, n_dom)
-        for j in range(per):
-            stage[r * per + j] = own[lists[r, j]]
-        if r == 0:
-            pl.semaphore_wait(barrier, rounds + n_col - 1)
-        copy = pltpu.make_async_remote_copy(
-            src_ref=stage.at[pl.ds(r * per, per)],
-            dst_ref=ext.at[pl.ds(blocks + r * per, per)],
-            send_sem=z_send.at[r], recv_sem=z_recv.at[r],
+        return pltpu.make_async_remote_copy(
+            src_ref=stage.at[h, pl.ds(r * per, per)],
+            dst_ref=exts[h].at[pl.ds(blocks + r * per, per)],
+            send_sem=z_send.at[h, r], recv_sem=z_recv.at[h, r],
             device_id={"dom": target}, device_id_type=MESH,
         )
-        copy.start()
-        z_copies.append(copy)
+
+    order = list(range(rounds))
+    for r in order:
+        for j in range(per):
+            block = own[lists[r, j]]
+            stage[0, r * per + j] = block[:part]
+            stage[1, r * per + j] = block[part:]
+        if r == order[0]:
+            pl.semaphore_wait(barrier, rounds + n_col - 1)
+        z_copy(0, r).start()
 
     def col_copy(at, d, here, send_sem, recv_sem):
         return pltpu.make_async_remote_copy(
@@ -106,27 +114,41 @@
     turned = w[...].reshape(width, -1).astype(F32).T.astype(BF)
     wt[...] = turned.reshape(wt.shape)
 
+    for r in order:
+        z_copy(0, r).wait_send()
+        z_copy(1, r).start()
     load_tiles.wait()
-    for copy in z_copies:
-        copy.wait()
 
     step = blocks // CHUNKS
     span = step * size
-    for i in range(CHUNKS):
-        def one(k, carry):
-            b = i * step + k
-            count = counts[b]
-            picked = jnp.concatenate(
-                [ext[jnp.where(t < count, cols[b, t], ext_total)] for t in range(slots)], axis=1
-            )
-            rows = jnp.concatenate([tiles[b, t] for t in range(slots)], axis=1)
-            total = nt_dot(picked, rows).astype(BF)
-            agg[i, c, :, pl.ds(pl.multiple_of(k * size, size), size)] = total
-            return carry
-
-        lax.fori_loop(0, step, one, 0)
-        for d in range(1, n_col):
-            col_copy(lambda q: agg.at[i, q], d, c, a_send.at[i, d - 1], a_recv.at[i, d - 1]).start()
+
+    def agg_part(i, h):
+        return lambda q: agg.at[i, q, pl.ds(h * part, part)]
+
+    for h in range(2):
+        ext = exts[h]
+        for r in order:
+            z_copy(h, r).wait_recv()
+            if h == 1:
+                z_copy(h, r).wait_send()
+        for i in range(CHUNKS):
+            def one(k, carry):
+                b = i * step + k
+                count = counts[b]
+                picked = jnp.concatenate(
+                    [ext[jnp.where(t < count, cols[b, t], ext_total)] for t in range(slots)], axis=1
+                )
+                rows = jnp.concatenate([tiles[b, t] for t in range(slots)], axis=1)
+                total = nt_dot(picked, rows).astype(BF)
+                columns = pl.ds(pl.multiple_of(k * size, size), size)
+                agg[i, c, h * part : (h + 1) * part, columns] = total
+                return carry
+
+            lax.fori_loop(0, step, one, 0)
+            for d in range(1, n_col):
+                col_copy(
+                    agg_part(i, h), d, c, a_send.at[h, i, d - 1], a_recv.at[h, i, d - 1]
+                ).start()
 
     for d in range(1, n_col):
         col_wait(lambda q: cot.at[q], d, c_send.at[d - 1], c_recv.at[d - 1])
@@ -134,7 +156,8 @@
     gw = jnp.zeros((feat, width), F32)
     for i in range(CHUNKS):
         for d in range(1, n_col):
-            col_wait(lambda q: agg.at[i, q], d, a_send.at[i, d - 1], a_recv.at[i, d - 1])
+            for h in range(2):
+                col_wait(agg_part(i, h), d, a_send.at[h, i, d - 1], a_recv.at[h, i, d - 1])
         whole = agg[i].reshape(width, span)
         pre = nn_dot(wt[...].reshape(width, width), whole)
         sigma = jax.nn.sigmoid(pre)
@@ -179,9 +202,10 @@
 def return_kernel(
     reduce_here, lists, ext_hbm, own, gw,
     out_ref, gw_out,
-    got0, got1, got2, got3, got4, got5, got6, got7, parts, sums,
-    z_send, z_recv, p_send, p_recv, s_send, s_recv, local_sem,
+    got0, got1, got2, got3, got4, got5, got6, got7, lane_in, lane_sum, layer_in, sums,
+    z_send, z_recv, a0, a1, b0, b1, c0, c1, d0, d1,
 ):
+    sem_a, sem_b, sem_c, sem_d = (a0, a1), (b0, b1), (c0, c1), (d0, d1)
     got = [got0, got1, got2, got3, got4, got5, got6, got7]
     n_dom = lax.axis_size("dom")
     me = lax.axis_index("dom")
@@ -191,42 +215,83 @@
     def peer(distance):
         return lax.rem(me + distance + n_dom, n_dom)
 
+    layers = n_dom // LANES
+    layer = me // LANES
+    lane = lax.rem(me, LANES)
+    near = {round_offset(r) % n_dom for r in range(rounds)}
+    if reduce_here:
+        near |= {d * LANES for d in range(1, layers)}
+        near |= {d % n_dom for d in range(1 - LANES, LANES) if d}
+    near = sorted(near)
     barrier = pltpu.get_barrier_semaphore()
-    if reduce_here:
-        def greet(d, carry):
-            pl.semaphore_signal(barrier, inc=1, device_id={"dom": peer(d)}, device_id_type=MESH)
-            return carry
-
-        lax.fori_loop(1, n_dom, greet, 0)
-    else:
-        for r in range(rounds):
-            pl.semaphore_signal(
-                barrier, inc=1, device_id={"dom": peer(round_offset(r))}, device_id_type=MESH
-            )
+    for d in near:
+        pl.semaphore_signal(barrier, inc=1, device_id={"dom": peer(d)}, device_id_type=MESH)
     for r in range(rounds):
         got[r][per] = jnp.zeros((feat, size), BF)
-    pl.semaphore_wait(barrier, n_dom - 1 if reduce_here else rounds)
-
-    def part_copy(d, target_slot, source_slot):
+    pl.semaphore_wait(barrier, len(near))
+
+    def lane_at(j):
+        return lax.rem(lane + j + LANES, LANES)
+
+    def layer_at(j):
+        return lax.rem(layer + j + layers, layers)
+
+    def dom_copy(src, dst, sems, j, target):
         return pltpu.make_async_remote_copy(
-            src_ref=gw.at[source_slot], dst_ref=parts.at[target_slot],
-            send_sem=p_send.at[d], recv_sem=p_recv.at[d],
-            device_id={"dom": peer(d)}, device_id_type=MESH,
+            src_ref=src, dst_ref=dst, send_sem=sems[0].at[j], recv_sem=sems[1].at[j],
+            device_id={"dom": target}, device_id_type=MESH,
         )
 
-    def sum_copy(d, slot):
-        return pltpu.make_async_remote_copy(
-            src_ref=sums.at[slot], dst_ref=sums.at[slot],
-            send_sem=s_send.at[d], recv_sem=s_recv.at[d],
-            device_id={"dom": peer(d)}, device_id_type=MESH,
-        )
-
+    def lane_device(j):
+        return layer * LANES + lane_at(j)
+
+    def layer_device(j):
+        return layer_at(j) * LANES + lane
+
+    def first(j):
+        return dom_copy(gw.at[lane_at(j)], lane_in.at[j], sem_a, j, lane_device(j))
+
+    def second(j):
+        return dom_copy(lane_sum.at[layer_at(j)], layer_in.at[j], sem_b, j, layer_device(j))
+
+    def third(j, at):
+        return dom_copy(sums.at[lane, at], sums.at[lane, at], sem_c, j, layer_device(j))
+
+    def fourth(j, at):
+        return dom_copy(sums.at[at], sums.at[at], sem_d, j, lane_device(j))
+
+    def stage_one():
+        for j in range(1, LANES):
+            first(j).start()
+
+    def stage_two():
+        total = gw[lane]
+        for j in range(1, LANES):
+            first(j).wait()
+            total = total + lane_in[j]
+        lane_sum[...] = total
+        for j in range(1, layers):
+            second(j).start()
+
+    def stage_three():
+        total = lane_sum[layer]
+        for j in range(1, layers):
+            second(j).wait()
+            total = total + layer_in[j]
+        sums[lane, layer] = total
+        for j in range(1, layers):
+            third(j, layer).start()
+
+    def stage_four():
+        for j in range(1, layers):
+            third(j, layer).wait_send()
+            third(j, layer_at(-j)).wait_recv()
+        for j in range(1, LANES):
+            fourth(j, lane).start()
+
+    stages = {0: stage_two, 2: stage_three, 4: stage_four} if reduce_here else {}
     if reduce_here:
-        def send_part(d, carry):
-            part_copy(d, d, peer(d)).start()
-            return carry
-
-        lax.fori_loop(1, n_dom, send_part, 0)
+        stage_one()
 
     copies = []
     for r in range(rounds):
@@ -239,20 +304,9 @@
         copy.start()
         copies.append(copy)
 
-    if reduce_here:
-        def wait_part(d, total):
-            part_copy(d, d, peer(d)).wait()
-            return total + parts[d]
-
-        sums[me] = lax.fori_loop(1, n_dom, wait_part, gw[me])
-
-        def send_sum(d, carry):
-            sum_copy(d, me).start()
-            return carry
-
-        lax.fori_loop(1, n_dom, send_sum, 0)
-
     for r in range(rounds):
+        if r in stages:
+            stages[r]()
         copies[r].wait()
 
         def add(b, carry):
@@ -267,15 +321,12 @@
         lax.fori_loop(0, blocks, add, 0)
 
     if reduce_here:
-        def wait_sum(d, carry):
-            sum_copy(d, me).wait_send()
-            sum_copy(d, peer(-d)).wait_recv()
-            return carry
-
-        lax.fori_loop(1, n_dom, wait_sum, 0)
-        flat = sums[...].reshape(-1, sums.shape[2])
+        for j in range(1, LANES):
+            fourth(j, lane).wait_send()
+            fourth(j, lane_at(-j)).wait_recv()
+        half = sums.shape[3]
+        flat = sums[...].reshape(-1, half)
         feat_rows = gw_out.shape[0]
-        half = sums.shape[2]
         for h in range(gw_out.shape[1] // half):
             gw_out[:, h * half : (h + 1) * half] = flat[h * feat_rows : (h + 1) * feat_rows]
     else:
@@ -308,21 +359,22 @@
         out_specs=(vmem, vmem, vmem),
         scratch_shapes=[
             pltpu.VMEM((blocks, feat, size), BF),
-            pltpu.VMEM((extra, feat, size), BF),
-            pltpu.VMEM((blocks + extra + 1, feat, size), BF),
+            pltpu.VMEM((2, extra, feat // 2, size), BF),
+            pltpu.VMEM((blocks + extra + 1, feat // 2, size), BF),
+            pltpu.VMEM((blocks + extra + 1, feat // 2, size), BF),
             pltpu.VMEM(tiles.shape, BF),
             pltpu.VMEM((n_col, feat, nodes), BF),
             pltpu.VMEM((n_col, feat, width), BF),
             pltpu.VMEM((n_col, feat, width), BF),
             pltpu.VMEM((CHUNKS, n_col, feat, span), BF),
-            dma((rounds,)), dma((rounds,)),
+            dma((2, rounds)), dma((2, rounds)),
             dma((n_col - 1,)), dma((n_col - 1,)),
             dma((n_col - 1,)), dma((n_col - 1,)),
-            dma((CHUNKS, n_col - 1)), dma((CHUNKS, n_col - 1)),
+            dma((2, CHUNKS, n_col - 1)), dma((2, CHUNKS, n_col - 1)),
             dma((3,)),
         ],
         compiler_params=pltpu.CompilerParams(
-            collective_id=0, has_side_effects=True, vmem_limit_bytes=40 * 2**20
+            collective_id=0, has_side_effects=True, vmem_limit_bytes=60 * 2**20
         ),
         name="forward",
     )(tile_cols, tile_count, lists, feats_t, cotangent_t, weight, tiles)
@@ -345,15 +397,16 @@
             pl.BlockSpec((extra, feat, size), lambda i: (0, 0, 0)),
         ),
         scratch_shapes=[pltpu.VMEM((blocks + extra + 1, feat, size), F32)],
-        compiler_params=pltpu.CompilerParams(vmem_limit_bytes=32 * 2**20),
+        compiler_params=pltpu.CompilerParams(vmem_limit_bytes=60 * 2**20),
         name="scatter",
     )(tile_cols, tile_count, gagg, tiles)
 
     total_rows = feat * (width // half)
-    reduce_here = total_rows % n_dom == 0 and (total_rows // n_dom) % 8 == 0
+    reduce_here = n_dom % LANES == 0 and total_rows % n_dom == 0 and (total_rows // n_dom) % 8 == 0
     rows = total_rows // n_dom if reduce_here else 8
-    parts_n = n_dom if reduce_here else 1
-    gw_in = gw.reshape(n_dom, rows, half) if reduce_here else jnp.zeros((1, 8, half), F32)
+    layers = n_dom // LANES if reduce_here else 1
+    gw_in = gw if reduce_here else jnp.zeros((LANES * rows, half), F32)
+    gw_in = gw_in.reshape(LANES, layers, rows, half)
     grad_feats_t, grad_weight = pl.pallas_call(
         functools.partial(return_kernel, reduce_here),
         out_shape=(
@@ -364,15 +417,18 @@
         out_specs=(vmem, vmem),
         scratch_shapes=[pltpu.VMEM((per + 1, feat, size), BF)] * rounds
         + [
-            pltpu.VMEM((parts_n, rows, half), F32),
-            pltpu.VMEM((parts_n, rows, half), F32),
+            pltpu.VMEM((LANES, layers, rows, half), F32),
+            pltpu.VMEM((layers, rows, half), F32),
+            pltpu.VMEM((layers, rows, half), F32),
+            pltpu.VMEM((LANES, layers, rows, half), F32),
             dma((rounds,)), dma((rounds,)),
-            dma((n_dom,)), dma((n_dom,)),
-            dma((n_dom,)), dma((n_dom,)),
-            dma((1,)),
+            dma((LANES,)), dma((LANES,)),
+            dma((layers,)), dma((layers,)),
+            dma((layers,)), dma((layers,)),
+            dma((LANES,)), dma((LANES,)),
         ],
         compiler_params=pltpu.CompilerParams(
-            collective_id=1, has_side_effects=True, vmem_limit_bytes=24 * 2**20
+            collective_id=1, has_side_effects=True, vmem_limit_bytes=48 * 2**20
         ),
         name="give_back",
     )(lists, ext, own, gw_in)

time: 106 us -> 102 us (0.962)
  local copies, waits for them, and re-layouts: 9.63 us -> 6.6 us
    pallas_call x1, Pallas kernels: 50.7 us -> 46.6 us  [shards(): pl.pallas_call(forward_kernel, out_shape=(jax.ShapeDtypeStruct((feat, nod...]
    pallas_call x1, Pallas kernels: 3.15 us -> 6.46 us  [shards(): pl.pallas_call(scatter_kernel, grid=(CHUNKS,), out_shape=(jax.ShapeDtypeS...]
    unnamed x16 -> x14, local copies, waits for them, and re-layouts: 9.63 us -> 6.6 us
where the time goes in v2:
time: 102 us
  Pallas kernels  94.3 us (92%)
  local copies, waits for them, and re-layouts  6.6 us (6%)
    pallas_call x1, Pallas kernels, shards(): pl.pallas_call(forward_kernel, out_shape=(jax.ShapeDtypeStruct((feat, nod...  46.6 us
    pallas_call x1, Pallas kernels, shards(): pl.pallas_call(functools.partial(return_kernel, reduce_here), out_shape=(...  41.3 us
    unnamed x14, local copies, waits for them, and re-layouts  6.6 us
    pallas_call x1, Pallas kernels, shards(): pl.pallas_call(scatter_kernel, grid=(CHUNKS,), out_shape=(jax.ShapeDtypeS...  6.46 us

profile of v2, /device:TPU:0, one launch (start us, length us, event | category | flops | bytes accessed | tf_op | source)
XLA Modules:
  0.0 101.6 jit_solution(6078369436520052356)
XLA Ops:
  0.6 1.4 %copy.10.cols = s32[16,8]{1,0:T(8,128)} copy(s32[16,8]{0,1:T(8,128)} %param.11) | data formatting | bytes 1024 | tf_op args[4]
  2.0 0.0 copy-start.3
  2.0 46.6 %forward.1 = (bf16[128,2048]{1,0:T(8,128)(2,1)}, bf16[16,128,128]{2,1,0:T(8,128)(2,1)}, f32[256,128]{1,0:T(8,128)}) custom-call(s32[16,8]{1,0:T(8,128)} %copy.10.cols, s32[16]{0:T(128)} %counts.3, s32[8,8]{1,0:T(8,128)} %bitcast.3, bf16[128,2048]{1,0:T(8,128)(2,1)} %feats.1, bf16[128,2048]{1,0:T(8,128)(2,1)} %cot_hbm.1, bf16[128,256]{1,0:T(8,128)(2,1)} %w_hbm.1, ...), custom_call_target="tpu_custom_call" | custom-call | tf_op jit(solution)/shard_map/forward/pallas_call | solution.py:351
  48.6 0.0 copy-start.2
  48.6 0.0 copy-start.4
  48.6 6.5 %scatter.1 = (f32[16,128,128]{2,1,0:T(8,128)}, bf16[64,128,128]{2,1,0:T(8,128)(2,1)}) custom-call(s32[16,8]{1,0:T(8,128)} %copy.10.cols, s32[16]{0:T(128)} %counts.3, bf16[16,128,128]{2,1,0:T(8,128)(2,1)} %get-tuple-element.11.gagg, bf16[16,8,128,128]{3,2,1,0:T(8,128)(2,1)} %tiles.1), custom_call_target="tpu_custom_call" | custom-call | tf_op jit(solution)/shard_map/scatter/pallas_call | solution.py:383
  55.0 0.0 copy-done.3
  55.0 0.0 copy-done.2
  55.0 0.0 copy-start
  55.0 1.6 %copy-done = bf16[64,128,128]{2,1,0:T(8,128)(2,1)S(1)} copy-done((bf16[64,128,128]{2,1,0:T(8,128)(2,1)S(1)}, bf16[64,128,128]{2,1,0:T(8,128)(2,1)}, u32[]{:S(2)}) %copy-start) | copy-done | bytes 2097176
  56.6 0.0 copy-start.1
  56.6 1.2 %copy-done.1 = f32[16,128,128]{2,1,0:T(8,128)S(1)} copy-done((f32[16,128,128]{2,1,0:T(8,128)S(1)}, f32[16,128,128]{2,1,0:T(8,128)}, u32[]{:S(2)}) %copy-start.1) | copy-done | bytes 1048600
  57.9 41.3 %give_back.1 = (f32[128,2048]{1,0:T(8,128)S(1)}, f32[128,256]{1,0:T(8,128)S(1)}) custom-call(s32[8,8]{1,0:T(8,128)S(1)} %bitcast.4, bf16[64,128,128]{2,1,0:T(8,128)(2,1)S(1)} %copy-done, f32[16,128,128]{2,1,0:T(8,128)S(1)} %copy-done.1, f32[4,4,16,128]{3,2,1,0:T(8,128)S(1)} %bitcast.2), custom_call_target="tpu_custom_call" | custom-call | tf_op jit(solution)/shard_map/give_back/pallas_call | solution.py:410
  99.2 0.0 copy-done.4
  99.2 0.8 copy.15
  100.0 0.7 copy.16
  100.7 1.0 copy.17
Async XLA Ops:
  2.0 53.0 %copy-start.3 = (s32[1,8,8]{2,1,0:T(8,128)S(1)}, s32[1,8,8]{2,1,0:T(8,128)}, u32[]{:S(2)}) copy-start(s32[1,8,8]{2,1,0:T(8,128)} %param.13) | copy-start | bytes 772
  48.6 6.5 %copy-start.2 = (f32[256,128]{1,0:T(8,128)S(1)}, f32[256,128]{1,0:T(8,128)}, u32[]{:S(2)}) copy-start(f32[256,128]{1,0:T(8,128)} %get-tuple-element.14) | copy-start | bytes 393220
  48.6 50.6 %copy-start.4 = (bf16[128,2048]{1,0:T(8,128)(2,1)S(1)}, bf16[128,2048]{1,0:T(8,128)(2,1)}, u32[]{:S(2)}) copy-start(bf16[128,2048]{1,0:T(8,128)(2,1)} %get-tuple-element.20) | copy-start | bytes 1572868
  55.0 1.6 %copy-start = (bf16[64,128,128]{2,1,0:T(8,128)(2,1)S(1)}, bf16[64,128,128]{2,1,0:T(8,128)(2,1)}, u32[]{:S(2)}) copy-start(bf16[64,128,128]{2,1,0:T(8,128)(2,1)} %get-tuple-element.12.ext_hbm) | copy-start | bytes 6291460
  56.6 1.2 %copy-start.1 = (f32[16,128,128]{2,1,0:T(8,128)S(1)}, f32[16,128,128]{2,1,0:T(8,128)}, u32[]{:S(2)}) copy-start(f32[16,128,128]{2,1,0:T(8,128)} %get-tuple-element.13.own) | copy-start | bytes 3145732

commit v3 on v2

--- a/solution.py
+++ b/solution.py
@@ -17,6 +17,10 @@
 def round_offset(round_index):
     step_size = round_index // 2 + 1
     return step_size if round_index % 2 == 0 else -step_size
+
+
+def farthest_first(rounds):
+    return sorted(range(rounds), key=lambda r: -abs(round_offset(r)))
 
 
 def nt_dot(a, b):
@@ -81,7 +85,7 @@
             device_id={"dom": target}, device_id_type=MESH,
         )
 
-    order = list(range(rounds))
+    order = farthest_first(rounds)
     for r in order:
         for j in range(per):
             block = own[lists[r, j]]
@@ -136,7 +140,7 @@
                 b = i * step + k
                 count = counts[b]
                 picked = jnp.concatenate(
-                    [ext[jnp.where(t < count, cols[b, t], ext_total)] for t in range(slots)], axis=1
+                    [ext[jnp.where(t < count, cols[t, b], ext_total)] for t in range(slots)], axis=1
                 )
                 rows = jnp.concatenate([tiles[b, t] for t in range(slots)], axis=1)
                 total = nt_dot(picked, rows).astype(BF)
@@ -190,7 +194,7 @@
         count = counts[b]
         grad = gagg[k]
         for t in range(slots):
-            at = jnp.where(t < count, cols[b, t], total)
+            at = jnp.where(t < count, cols[t, b], total)
             acc[at] += nn_dot(grad, tiles[k, t])
 
     @pl.when(step == pl.num_programs(0) - 1)
@@ -293,8 +297,9 @@
     if reduce_here:
         stage_one()
 
-    copies = []
-    for r in range(rounds):
+    copies = {}
+    order = farthest_first(rounds)
+    for r in order:
         copy = pltpu.make_async_remote_copy(
             src_ref=ext_hbm.at[pl.ds(r * per, per)],
             dst_ref=got[r].at[pl.ds(0, per)],
@@ -302,11 +307,11 @@
             device_id={"dom": peer(-round_offset(r))}, device_id_type=MESH,
         )
         copy.start()
-        copies.append(copy)
-
-    for r in range(rounds):
-        if r in stages:
-            stages[r]()
+        copies[r] = copy
+
+    for place, r in enumerate(order):
+        if place in stages:
+            stages[place]()
         copies[r].wait()
 
         def add(b, carry):
@@ -314,7 +319,7 @@
             for j in range(per):
                 at = jnp.where(lists[r, j] == b, j, at)
             columns = pl.ds(pl.multiple_of(b * size, size), size)
-            base = own[b] if r == 0 else out_ref[:, columns]
+            base = own[b] if place == 0 else out_ref[:, columns]
             out_ref[:, columns] = base + got[r][at].astype(F32)
             return carry
 
@@ -340,6 +345,7 @@
     rounds, per = send_blocks.shape[1:]
     extra = rounds * per
     lists = send_blocks[0]
+    slot_cols = tile_cols.T
     step = blocks // CHUNKS
     span = step * size
     vmem = pl.BlockSpec(memory_space=pltpu.VMEM)
@@ -377,7 +383,7 @@
             collective_id=0, has_side_effects=True, vmem_limit_bytes=60 * 2**20
         ),
         name="forward",
-    )(tile_cols, tile_count, lists, feats_t, cotangent_t, weight, tiles)
+    )(slot_cols, tile_count, lists, feats_t, cotangent_t, weight, tiles)
 
     per_step = blocks // CHUNKS
     own, ext = pl.pallas_call(
@@ -397,9 +403,9 @@
             pl.BlockSpec((extra, feat, size), lambda i: (0, 0, 0)),
         ),
         scratch_shapes=[pltpu.VMEM((blocks + extra + 1, feat, size), F32)],
-        compiler_params=pltpu.CompilerParams(vmem_limit_bytes=60 * 2**20),
+        compiler_params=pltpu.CompilerParams(vmem_limit_bytes=32 * 2**20),
         name="scatter",
-    )(tile_cols, tile_count, gagg, tiles)
+    )(slot_cols, tile_count, gagg, tiles)
 
     total_rows = feat * (width // half)
     reduce_here = n_dom % LANES == 0 and total_rows % n_dom == 0 and (total_rows // n_dom) % 8 == 0

time: 102 us -> 98 us (0.961)
  Pallas kernels: 94.3 us -> 91.4 us
    pallas_call x1, Pallas kernels: 6.46 us -> 3.09 us  [shards(): pl.pallas_call(scatter_kernel, grid=(CHUNKS,), out_shape=(jax.ShapeDtypeS...]
    unnamed x14 -> x17, local copies, waits for them, and re-layouts: 6.6 us -> 5.66 us
where the time goes in v3:
time: 98 us; the launch traced here: 97.8 us
  Pallas kernels  91.4 us (93%)
  local copies, waits for them, and re-layouts  5.66 us (6%)
    pallas_call x1, Pallas kernels, shards(): pl.pallas_call(forward_kernel, out_shape=(jax.ShapeDtypeStruct((feat, nod...  46.5 us
    pallas_call x1, Pallas kernels, shards(): pl.pallas_call(functools.partial(return_kernel, reduce_here), out_shape=(...  41.8 us
    unnamed x17, local copies, waits for them, and re-layouts  5.66 us
    pallas_call x1, Pallas kernels, shards(): pl.pallas_call(scatter_kernel, grid=(CHUNKS,), out_shape=(jax.ShapeDtypeS...  3.09 us

profile of v3, /device:TPU:0, one launch (start us, length us, event | category | flops | bytes accessed | tf_op | source)
XLA Modules:
  0.0 97.8 jit_solution(1324349484940800303)
XLA Ops:
  0.6 0.0 copy-start.5
  0.6 0.0 copy-start.4
  0.7 0.0 copy-start.3
  0.7 46.5 %forward.1 = (bf16[128,2048]{1,0:T(8,128)(2,1)}, bf16[16,128,128]{2,1,0:T(8,128)(2,1)}, f32[256,128]{1,0:T(8,128)}) custom-call(s32[8,16]{1,0:T(8,128)} %bitcast.6, s32[16]{0:T(128)} %counts.3, s32[8,8]{1,0:T(8,128)} %bitcast.4, bf16[128,2048]{1,0:T(8,128)(2,1)} %feats.1, bf16[128,2048]{1,0:T(8,128)(2,1)} %cot_hbm.1, bf16[128,256]{1,0:T(8,128)(2,1)} %w_hbm.1, ...), custom_call_target="tpu_custom_call" | custom-call | tf_op jit(solution)/shard_map/forward/pallas_call | solution.py:357
  47.1 0.0 copy-done.5
  47.1 0.0 copy-done.4
  47.1 0.0 copy-start
  47.2 2.2 %copy-done = bf16[16,8,128,128]{3,2,1,0:T(8,128)(2,1)S(1)} copy-done((bf16[16,8,128,128]{3,2,1,0:T(8,128)(2,1)S(1)}, bf16[16,8,128,128]{3,2,1,0:T(8,128)(2,1)}, u32[]{:S(2)}) %copy-start) | copy-done | bytes 4194328
  49.3 0.0 copy-start.1
  49.3 1.0 %copy-done.1 = bf16[16,128,128]{2,1,0:T(8,128)(2,1)S(1)} copy-done((bf16[16,128,128]{2,1,0:T(8,128)(2,1)S(1)}, bf16[16,128,128]{2,1,0:T(8,128)(2,1)}, u32[]{:S(2)}) %copy-start.1) | copy-done | bytes 524312
  50.4 0.0 copy-start.2
  50.4 0.0 copy-start.6
  50.4 3.1 %scatter.1 = (f32[16,128,128]{2,1,0:T(8,128)S(1)}, bf16[64,128,128]{2,1,0:T(8,128)(2,1)S(1)}) custom-call(s32[8,16]{1,0:T(8,128)S(1)} %bitcast.7, s32[16]{0:T(128)S(1)} %copy-done.5, bf16[16,128,128]{2,1,0:T(8,128)(2,1)S(1)} %copy-done.1, bf16[16,8,128,128]{3,2,1,0:T(8,128)(2,1)S(1)} %copy-done), custom_call_target="tpu_custom_call" | custom-call | tf_op jit(solution)/shard_map/scatter/pallas_call | solution.py:389
  53.5 0.0 copy-done.3
  53.5 0.0 copy-done.2
  53.5 41.8 %give_back.1 = (f32[128,2048]{1,0:T(8,128)S(1)}, f32[128,256]{1,0:T(8,128)S(1)}) custom-call(s32[8,8]{1,0:T(8,128)S(1)} %bitcast.5, bf16[64,128,128]{2,1,0:T(8,128)(2,1)S(1)} %get-tuple-element.12.ext_hbm, f32[16,128,128]{2,1,0:T(8,128)S(1)} %get-tuple-element.13.own, f32[4,4,16,128]{3,2,1,0:T(8,128)S(1)} %bitcast.3), custom_call_target="tpu_custom_call" | custom-call | tf_op jit(solution)/shard_map/give_back/pallas_call | solution.py:416
  95.3 0.0 copy-done.6
  95.4 0.8 copy.13
  96.2 0.7 copy.14
  96.8 1.0 copy.15
Async XLA Ops:
  0.6 46.5 %copy-start.5 = (s32[16]{0:T(128)S(1)}, s32[16]{0:T(128)}, u32[]{:S(2)}) copy-start(s32[16]{0:T(128)} %counts.3) | copy-start | bytes 196
  0.6 46.5 %copy-start.4 = (s32[16,8]{0,1:T(8,128)S(1)}, s32[16,8]{0,1:T(8,128)}, u32[]{:S(2)}) copy-start(s32[16,8]{0,1:T(8,128)} %param.11) | copy-start | bytes 1540
  0.7 52.8 %copy-start.3 = (s32[1,8,8]{2,1,0:T(8,128)S(1)}, s32[1,8,8]{2,1,0:T(8,128)}, u32[]{:S(2)}) copy-start(s32[1,8,8]{2,1,0:T(8,128)} %param.13) | copy-start | bytes 772
  47.1 2.2 %copy-start = (bf16[16,8,128,128]{3,2,1,0:T(8,128)(2,1)S(1)}, bf16[16,8,128,128]{3,2,1,0:T(8,128)(2,1)}, u32[]{:S(2)}) copy-start(bf16[16,8,128,128]{3,2,1,0:T(8,128)(2,1)} %tiles.1) | copy-start | bytes 12582916
  49.3 1.0 %copy-start.1 = (bf16[16,128,128]{2,1,0:T(8,128)(2,1)S(1)}, bf16[16,128,128]{2,1,0:T(8,128)(2,1)}, u32[]{:S(2)}) copy-start(bf16[16,128,128]{2,1,0:T(8,128)(2,1)} %get-tuple-element.11.gagg) | copy-start | bytes 1572868
  50.4 3.1 %copy-start.2 = (f32[256,128]{1,0:T(8,128)S(1)}, f32[256,128]{1,0:T(8,128)}, u32[]{:S(2)}) copy-start(f32[256,128]{1,0:T(8,128)} %get-tuple-element.14) | copy-start | bytes 393220
  50.4 45.0 %copy-start.6 = (bf16[128,2048]{1,0:T(8,128)(2,1)S(1)}, bf16[128,2048]{1,0:T(8,128)(2,1)}, u32[]{:S(2)}) copy-start(bf16[128,2048]{1,0:T(8,128)(2,1)} %get-tuple-element.20) | copy-start | bytes 1572868
